TPU v7x, 512 devices: a whole 4x8x8 slice. The times are simulated.
512 devices in a mesh: dp: 32 (over x, y), space: 16 (over z, core).
Axes of the slice: x: 4, y: 8, z: 8, core: 2. Of those that a mesh axis runs over, the one named last changes fastest.
Arguments:
- features: bfloat16 [32, 512, 64, 256], P('dp', 'space'), may hold values from -6 to 6
- cotangent: bfloat16 [32, 256, 64, 256], P('dp', 'space'), may hold values from -6 to 6
- weights: bfloat16 [7, 256, 256], replicated, may hold values from -0.125 to 0.125
- counts: int32 [32, 16], P('dp', 'space'), may hold values from 0 to 32, as said below
- neighbours: int32 [32, 512, 6], P('dp', 'space'), may hold values from 0 to 96, as said below
- send_list: int32 [32, 16, 16, 2], P('dp', 'space'), may hold values from 0 to 32, as said below
- recv_list: int32 [32, 256], P('dp', 'space'), may hold values from 0 to 31, as said below
Outputs:
- voxel_out: bfloat16 [32, 512, 64, 256], P('dp', 'space')
- weight_grad: bfloat16 [7, 256, 256], replicated
Inputs may be any that keep to these rules, and one draw needn't show every extreme that they name: The live slots of an owner are its first counts slots; the counts of one scene sum to 16 times the number of space devices, and some owner of every scene holds 32. `send_list`: entry [g, s, j, c] is the c-th (rising) live Morton slot of owner s whose block goes to balanced owner j, or 32 past the last one; every live slot appears exactly once, at most 2 from one owner to one balanced owner, and an owner holding 32 sends exactly 2 to each. `recv_list`: entry [g, j * 16 + r] is s * 2 + c, naming the block that owner s sends as its c-th to balanced owner j; the entries of one balanced owner are distinct and cover all blocks sent to it, so every balanced owner holds exactly 16 blocks. `neighbours`: entries name live slots only; slots that are not live have none in every direction; only -x names the previous owner and only +x the next one.
All inputs are finite; a program needn't handle non-finite values.
Results may differ from a plain program's by a relative error of at most 0.012.
Values may be sent and summed in bfloat16 or wider, within the bound.
A program may use at most 64 MiB of HBM per device.

v0:
```python
import math

import jax
import jax.numpy as jnp
from jax import lax
from jax.sharding import PartitionSpec as P

BLOCK_VOXELS = 64


def with_halo(cells, sides, width):
    for axis, dim in sides:
        count = lax.axis_size(axis)
        ends = count - 1
        head = lax.slice_in_dim(cells, 0, width, axis=dim)
        tail = lax.slice_in_dim(cells, cells.shape[dim] - width, cells.shape[dim], axis=dim)
        cells = jnp.concatenate(
            [
                lax.ppermute(tail, axis, [(i, (i + 1) % count) for i in range(ends)]),
                cells,
                lax.ppermute(head, axis, [((i + 1) % count, i) for i in range(ends)]),
            ],
            axis=dim,
        )
    return cells


def plane_views(blocks):
    return [
        blocks[:, 3],
        blocks[:, 0],
        blocks[:, :, 3],
        blocks[:, :, 0],
        blocks[:, :, :, 3],
        blocks[:, :, :, 0],
    ]


def shifted_taps(blocks, faces):
    channels = blocks.shape[-1]
    tap_list = [
        blocks,
        jnp.concatenate([faces[0][:, None], blocks[:, :3]], 1),
        jnp.concatenate([blocks[:, 1:], faces[1][:, None]], 1),
        jnp.concatenate([faces[2][:, :, None], blocks[:, :, :3]], 2),
        jnp.concatenate([blocks[:, :, 1:], faces[3][:, :, None]], 2),
        jnp.concatenate([faces[4][:, :, :, None], blocks[:, :, :, :3]], 3),
        jnp.concatenate([blocks[:, :, :, 1:], faces[5][:, :, :, None]], 3),
    ]
    return jnp.stack(tap_list, 0).reshape(7, -1, channels)


def gather_faces(blocks, link_rows):
    slot_count = blocks.shape[0]
    channels = blocks.shape[-1]
    planes = plane_views(blocks)
    edge_planes = jnp.concatenate(
        [planes[1].reshape(slot_count, 16, channels), planes[0].reshape(slot_count, 16, channels)],
        0,
    )
    extended = with_halo(edge_planes, (("space", 0),), slot_count)
    from_left = extended[:slot_count]
    from_right = extended[3 * slot_count :]
    zero_face = jnp.zeros((1, 16, channels), blocks.dtype)
    gathered = []
    for direction in range(6):
        lookup = jnp.concatenate(
            [planes[direction].reshape(slot_count, 16, channels), from_left, from_right, zero_face],
            0,
        )
        gathered.append(lookup[link_rows[:, direction]].reshape(slot_count, 4, 4, channels))
    return gathered


def conv_terms(tap_rows, weights, cot_rows):
    conv_out = jnp.einsum("krc,kcd->rd", tap_rows, weights, preferred_element_type=jnp.float32)
    grad_term = jnp.einsum("krc,rd->kcd", tap_rows, cot_rows, preferred_element_type=jnp.float32)
    return (conv_out, grad_term)


def shards(features, cotangent, weights, counts, neighbours, send_list, recv_list):
    slot_count = features.shape[1]
    channels = features.shape[-1]
    balanced = cotangent.shape[1]
    peer_count = send_list.shape[2]
    capacity = send_list.shape[3]
    blocks = features[0].reshape(slot_count, 4, 4, 4, channels)
    faces = gather_faces(blocks, neighbours[0])
    packed_faces = jnp.stack(faces, 1).reshape(slot_count, 96, channels)
    tile_rows = jnp.concatenate([features[0], packed_faces], 1)
    tile_rows = jnp.concatenate([tile_rows, jnp.zeros((1, 160, channels), tile_rows.dtype)], 0)
    outgoing = tile_rows[send_list[0, 0]]
    incoming = lax.all_to_all(outgoing, "space", split_axis=0, concat_axis=0, tiled=True)
    gathered = incoming.reshape(peer_count * capacity, 160, channels)[recv_list[0]]
    own_blocks = gathered[:, :BLOCK_VOXELS].reshape(balanced, 4, 4, 4, channels)
    own_stack = gathered[:, BLOCK_VOXELS:].reshape(balanced, 6, 4, 4, channels)
    own_faces = [own_stack[:, direction] for direction in range(6)]
    tap_rows = shifted_taps(own_blocks, own_faces)
    conv_out, grad_term = conv_terms(tap_rows, weights, cotangent[0].reshape(-1, channels))
    answers = conv_out.astype(jnp.bfloat16).reshape(balanced, BLOCK_VOXELS, channels)
    returning = (
        jnp.zeros((peer_count * capacity, BLOCK_VOXELS, channels), jnp.bfloat16)
        .at[recv_list[0]]
        .set(answers)
    )
    arrived = lax.all_to_all(
        returning.reshape(peer_count, capacity, BLOCK_VOXELS, channels),
        "space",
        split_axis=0,
        concat_axis=0,
        tiled=True,
    )
    placed = jnp.zeros((slot_count + 1, BLOCK_VOXELS, channels), jnp.bfloat16)
    placed = placed.at[send_list[0, 0].reshape(-1)].set(
        arrived.reshape(peer_count * capacity, BLOCK_VOXELS, channels)
    )
    voxel_out = placed[:slot_count].reshape(1, slot_count, BLOCK_VOXELS, channels)
    summed = lax.psum(grad_term, ("dp", "space"))
    grad_scale = 1.0 / math.sqrt(
        lax.axis_size("dp") * lax.axis_size("space") * balanced * BLOCK_VOXELS
    )
    weight_grad = (summed * grad_scale).astype(jnp.bfloat16)
    return (voxel_out, weight_grad)


def solution(mesh):
    placed = (
        P("dp", "space", None, None),
        P("dp", "space", None, None),
        P(),
        P("dp", "space"),
        P("dp", "space", None),
        P("dp", "space", None, None),
        P("dp", "space"),
    )
    return jax.shard_map(
        shards,
        mesh=mesh,
        in_specs=placed,
        out_specs=(P("dp", "space", None, None), P()),
        check_vma=False,
    )
```

profile of v0, /device:TPU:1, one launch (start us, length us, event | category | flops | bytes accessed | tf_op | source)
XLA Modules:
  0.0 456.7 jit_solution(14949315525642156280)
XLA Ops:
  7.2 1.9 copy.38
  9.3 5.4 %collective-permute-start = (bf16[32,16,256]{2,1,0:T(8,128)(2,1)S(1)}, bf16[32,16,256]{2,1,0:T(8,128)(2,1)S(1)}, u32[]{:S(2)}, u32[]{:S(2)}) collective-permute-start(bf16[32,16,256]{2,1,0:T(8,128)(2,1)S(1)} %copy.62), channel_id=1, source_target_pairs={{0,1},{1,2},{2,3},{3,4},{4,5},{5,6},{6,7},{7,8},{8,9},{9,10},{10,1... | collective-permute-start | bytes 786440 | tf_op jit(solution)/shard_map/ppermute | solution.py:19
  14.9 4.7 %collective-permute-start.1 = (bf16[32,16,256]{2,1,0:T(8,128)(2,1)S(1)}, bf16[32,16,256]{2,1,0:T(8,128)(2,1)}, u32[]{:S(2)}, u32[]{:S(2)}) collective-permute-start(bf16[32,16,256]{2,1,0:T(8,128)(2,1)S(1)} %copy.63), channel_id=1, source_target_pairs={{1,0},{2,1},{3,2},{4,3},{5,4},{6,5},{7,6},{8,7},{9,8},{10,9},{11,1... | collective-permute-start | bytes 786440 | tf_op jit(solution)/shard_map/ppermute | solution.py:21
  22.7 2.8 fusion.9
  26.3 1.7 gather_fusion.1
  28.0 0.8 copy.65
  28.8 1.8 gather_fusion.2
  31.4 1.8 gather_fusion.3
  33.2 0.8 copy.69
  34.0 1.8 gather_fusion.4
  35.9 0.8 copy.70
  37.4 1.0 constant_dynamic-update-slice_fusion.4
  38.4 1.1 constant_dynamic-update-slice_fusion.3
  39.5 1.0 constant_dynamic-update-slice_fusion.2
  40.5 1.0 constant_dynamic-update-slice_fusion.1
  41.5 0.9 copy.51
  42.4 1.8 fusion.2
  44.2 4.0 gather_fusion.6
  48.2 9.9 %all-to-all-start = ((bf16[16,2,160,256]{3,2,1,0:T(8,128)(2,1)}), bf16[16,2,160,256]{3,2,1,0:T(8,128)(2,1)S(1)}, u32[]{:S(2)}, u32[]{:S(2)}) async-start(bf16[16,2,160,256]{3,2,1,0:T(8,128)(2,1)} %bitcast.25), calls=%async_computation | async-start | bytes 5242880 | tf_op jit(solution)/shard_map/all_to_all | solution.py:93
  58.2 59.8 %all-to-all-done = bf16[16,2,160,256]{3,2,1,0:T(8,128)(2,1)S(1)} async-done(((bf16[16,2,160,256]{3,2,1,0:T(8,128)(2,1)}), bf16[16,2,160,256]{3,2,1,0:T(8,128)(2,1)S(1)}, u32[]{:S(2)}, u32[]{:S(2)}) %all-to-all-start) | async-done | bytes 2621472 | tf_op jit(solution)/shard_map/all_to_all | solution.py:93
  117.9 1.7 gather_fusion.7
  119.6 1.1 slice.130
  121.4 1.2 fusion.22
  122.6 1.2 fusion.23
  124.2 0.9 slice_bitcast_fusion.1
  126.0 1.2 copy.58
  127.8 1.0 copy.57
  128.8 1.3 pad_maximum_fusion.15
  130.3 1.0 copy.56
  131.3 2.1 pad_maximum_fusion.14
  133.4 1.2 stack.30
  134.6 1.0 copy.55
  135.6 2.1 pad_maximum_fusion.13
  137.7 2.0 stack.29
  139.7 1.0 copy.54
  140.6 2.1 pad_maximum_fusion.12
  142.8 2.0 stack.28
  144.8 1.1 constant_dynamic-update-slice_fusion.11
  145.8 1.1 constant_dynamic-update-slice_fusion.10
  147.1 1.1 fusion.3
  148.9 1.1 broadcast_in_dim.7
  150.0 2.6 scatter_fusion
  152.6 5.4 %all-to-all-start.1 = ((bf16[16,2,64,256]{3,2,1,0:T(8,128)(2,1)}), bf16[16,2,64,256]{3,2,1,0:T(8,128)(2,1)S(1)}, u32[]{:S(2)}, u32[]{:S(2)}) async-start(bf16[16,2,64,256]{3,2,1,0:T(8,128)(2,1)} %bitcast.35), calls=%async_computation.1 | async-start | bytes 2097152 | tf_op jit(solution)/shard_map/all_to_all | solution.py:106
  158.0 4.4 fusion.24
  162.7 281.8 %all-reduce.3.cloned.1.call-done = f32[7,256,256]{2,1,0:T(8,128)} async-done(((f32[7,256,256]{2,1,0:T(8,128)}), f32[7,256,256]{2,1,0:T(8,128)}) %all-reduce.3.cloned.1.call-update) | async-done | bytes 1835024 | tf_op jit(solution)/shard_map/psum | solution.py:118
  444.5 2.6 multiply_convert_fusion
  447.2 1.6 scatter_fusion.1
  448.9 1.0 slice_bitcast_fusion
  (69 shorter events, 9.8 us)
Async XLA Ops:
  7.2 139.9 %copy-start = (bf16[7,256,256]{2,1,0:T(8,128)(2,1)S(1)}, bf16[7,256,256]{2,1,0:T(8,128)(2,1)}, u32[]{:S(2)}) copy-start(bf16[7,256,256]{2,1,0:T(8,128)(2,1)} %param.9) | copy-start | bytes 2752516
  9.1 10.6 %copy-start.5 = (s32[1,32,6]{1,0,2:T(1,128)S(1)}, s32[1,32,6]{1,0,2:T(1,128)}, u32[]{:S(2)}) copy-start(s32[1,32,6]{1,0,2:T(1,128)} %param.10) | copy-start | bytes 2308
  9.1 10.6 %copy-start.3 = (s32[1,1,16,2]{2,3,1,0:T(2,128)S(1)}, s32[1,1,16,2]{2,3,1,0:T(2,128)}, u32[]{:S(2)}) copy-start(s32[1,1,16,2]{2,3,1,0:T(2,128)} %param.11) | copy-start | bytes 388
  9.3 13.1 %collective-permute-start = (bf16[32,16,256]{2,1,0:T(8,128)(2,1)S(1)}, bf16[32,16,256]{2,1,0:T(8,128)(2,1)S(1)}, u32[]{:S(2)}, u32[]{:S(2)}) collective-permute-start(bf16[32,16,256]{2,1,0:T(8,128)(2,1)S(1)} %copy.62), channel_id=1, source_target_pairs={{0,1},{1,2},{2,3},{3,4},{4,5},{5,6},{6,7},{7,8},{8,9},{9,10},{10,1... | collective-permute-start | bytes 786440 | tf_op jit(solution)/shard_map/ppermute | solution.py:19
  14.9 7.8 %collective-permute-start.1 = (bf16[32,16,256]{2,1,0:T(8,128)(2,1)S(1)}, bf16[32,16,256]{2,1,0:T(8,128)(2,1)}, u32[]{:S(2)}, u32[]{:S(2)}) collective-permute-start(bf16[32,16,256]{2,1,0:T(8,128)(2,1)S(1)} %copy.63), channel_id=1, source_target_pairs={{1,0},{2,1},{3,2},{4,3},{5,4},{6,5},{7,6},{8,7},{9,8},{10,9},{11,1... | collective-permute-start | bytes 786440 | tf_op jit(solution)/shard_map/ppermute | solution.py:21
  38.4 3.9 copy-start.1
  48.2 9.9 %copy-start.7 = (s32[1,16]{1,0:T(1,128)S(1)}, s32[1,16]{1,0:T(1,128)}, u32[]{:S(2)}) copy-start(s32[1,16]{1,0:T(1,128)} %param.12) | copy-start | bytes 196
  48.2 69.7 %all-to-all-start = ((bf16[16,2,160,256]{3,2,1,0:T(8,128)(2,1)}), bf16[16,2,160,256]{3,2,1,0:T(8,128)(2,1)S(1)}, u32[]{:S(2)}, u32[]{:S(2)}) async-start(bf16[16,2,160,256]{3,2,1,0:T(8,128)(2,1)} %bitcast.25), calls=%async_computation | async-start | bytes 5242880 | tf_op jit(solution)/shard_map/all_to_all | solution.py:93
  120.8 2.9 slice-start
  147.1 1.8 copy-start.2
  148.9 9.1 %copy-start.6 = (bf16[1,16,64,256]{3,2,1,0:T(8,128)(2,1)S(1)}, bf16[1,16,64,256]{3,2,1,0:T(8,128)(2,1)}, u32[]{:S(2)}) copy-start(bf16[1,16,64,256]{3,2,1,0:T(8,128)(2,1)} %param.8) | copy-start | bytes 1572868
  152.6 294.6 %all-to-all-start.1 = ((bf16[16,2,64,256]{3,2,1,0:T(8,128)(2,1)}), bf16[16,2,64,256]{3,2,1,0:T(8,128)(2,1)S(1)}, u32[]{:S(2)}, u32[]{:S(2)}) async-start(bf16[16,2,64,256]{3,2,1,0:T(8,128)(2,1)} %bitcast.35), calls=%async_computation.1 | async-start | bytes 2097152 | tf_op jit(solution)/shard_map/all_to_all | solution.py:106
  157.9 286.6 %all-reduce.3.cloned.1.call-start = ((), (), s32[]{:S(2)}) async-start(), calls=%async_computation.2 | async-start | bytes 3670016 | tf_op jit(solution)/shard_map/psum | solution.py:118
  158.0 4.5 copy-start.4
Sparse Core Ops, SparseCore 0:
  163.7 280.7 all-reduce.2
where the time goes:
time: 458 us; the launch traced here: 457 us
  waiting for transfers between devices  342 us (75%)
  local copies, waits for them, and re-layouts  51.4 us (11%)
  starting transfers between devices  25.4 us (6%)
  other arithmetic  17.9 us (4%)
  between operations  14.5 us (3%)
  matrix products  5.57 us (1%)
    psum x1, waiting for transfers between devices, shards(): summed = lax.psum(grad_term, ('dp', 'space'))  282 us
    all_to_all x1, waiting for transfers between devices, shards(): lax.all_to_all(outgoing, 'space', split_axis=0, concat_axis=0, tiled=True)  59.8 us
    all_to_all x1, starting transfers between devices, shards(): lax.all_to_all(outgoing, 'space', split_axis=0, concat_axis=0, tiled=True)  9.94 us
  transfers between devices with their start and end apart: 5, of which 3 were waited for; matrix products, arithmetic and copies ran while one was open for 2% of the time, Pallas kernels for 0%

commit v1 on v0

v1 whole, which is shorter than its diff:
```python
import functools
import math

import jax
import jax.numpy as jnp
from jax import lax
from jax.experimental import pallas as pl
from jax.experimental.pallas import tpu as pltpu
from jax.sharding import PartitionSpec as P

MESH = pl.DeviceIdType.MESH
BV = 64
LANES = 128
PARTS = 2
F32 = jnp.float32
BF16 = jnp.bfloat16


def kernel(
    dims,
    cot_hbm, feat_hbm, w_hbm, counts_s, nbr_s, send_s, recv_s,
    out_hbm, wg_hbm,
    cot, feat, w, ext_m, ext_p, taps, taps_t, vout,
    outbuf, inbuf, acc,
    core_out, core_in, x_out, x_in, gx, y_out, y_in, zbuf, ybuf, cbuf,
    local_sem, halo_ss, halo_rs, cot_ss, cot_rs,
    core_ss, core_rs, x_ss, x_rs, y_ss, y_rs, z_ss, z_rs,
    yg_ss, yg_rs, xg_ss, xg_rs, cg_ss, cg_rs,
):
    nx, ny, nz, slots, bal, channels, scale = dims
    ns = 2 * nz
    taps_w = 7 * channels
    half = taps_w // 2
    xr = half // nx
    yr = gx.shape[0] // ny
    dp = lax.axis_index("dp")
    me = lax.axis_index("space")
    x, y = dp // ny, dp % ny
    z, core = me // 2, me % 2

    def remote(src, dst, ss, rs, dev):
        return pltpu.make_async_remote_copy(
            src_ref=src, dst_ref=dst, send_sem=ss, recv_sem=rs, device_id=dev, device_id_type=MESH
        )

    def space_peer(s):
        return (dp, s)

    def x_peer(d):
        return (lax.rem(x + d, nx) * ny + y, me)

    def y_peer(d):
        return (x * ny + lax.rem(y + d, ny), me)

    def z_peer(d):
        return (dp, lax.rem(z + d, nz) * 2 + core)

    sibling = (dp, z * 2 + (1 - core))

    barrier = pltpu.get_barrier_semaphore()

    @pl.loop(1, ns)
    def _(i):
        pl.semaphore_signal(barrier, inc=1, device_id=space_peer(lax.rem(me + i, ns)), device_id_type=MESH)

    @pl.loop(1, nx)
    def _(i):
        pl.semaphore_signal(barrier, inc=1, device_id=x_peer(i), device_id_type=MESH)

    @pl.loop(1, ny)
    def _(i):
        pl.semaphore_signal(barrier, inc=1, device_id=y_peer(i), device_id_type=MESH)

    load_cot = pltpu.make_async_copy(cot_hbm, cot, local_sem.at[0])
    load_feat = pltpu.make_async_copy(feat_hbm, feat.at[pl.ds(0, slots)], local_sem.at[1])
    load_w = pltpu.make_async_copy(w_hbm, w, local_sem.at[2])
    load_cot.start()
    load_feat.start()
    load_w.start()

    def offset(i):
        k = (i + 1) // 2
        return lax.rem(nz // 2 + k * (1 - 2 * lax.rem(i, 2)) + nz, nz)

    last = nz - 1

    feat[slots] = jnp.zeros((BV, channels), BF16)
    taps[slots] = jnp.zeros((BV, taps_w), BF16)
    ext_m[2 * slots] = jnp.zeros((16, channels), BF16)
    ext_p[2 * slots] = jnp.zeros((16, channels), BF16)

    load_cot.wait()

    @pl.loop(0, ns)
    def _(t):
        i, c = t // 2, lax.rem(t, 2)
        dest = lax.rem(z - offset(i) + nz, nz) * 2 + c
        for place in range(2):
            wanted = dest * 2 + place
            pos = jnp.int32(0)
            for r in range(bal):
                pos = jnp.where(recv_s[0, r] == wanted, r, pos)
            block = cot[pos]
            for h in range(PARTS):
                outbuf[h, i, c, pl.ds(place * BV, BV), :] = block[:, h * LANES : (h + 1) * LANES]

    load_feat.wait()

    @pl.loop(0, slots)
    def _(b):
        ext_m[b] = feat[b, 48:64, :]
        ext_p[b] = feat[b, 0:16, :]

    pl.semaphore_wait(barrier, ns - 1 + nx - 1 + ny - 1)

    halo_right = remote(
        ext_m.at[pl.ds(0, slots)], ext_m.at[pl.ds(slots, slots)], halo_ss.at[0], halo_rs.at[0],
        space_peer(lax.rem(me + 1, ns)),
    )
    halo_left = remote(
        ext_p.at[pl.ds(0, slots)], ext_p.at[pl.ds(slots, slots)], halo_ss.at[1], halo_rs.at[1],
        space_peer(lax.rem(me + ns - 1, ns)),
    )
    halo_right.start()
    halo_left.start()

    def cot_copy(h, i, c):
        dest = lax.rem(z - offset(i) + nz, nz) * 2 + c
        return remote(outbuf.at[h, i, c], inbuf.at[h, i, core], cot_ss.at[h, i, c], cot_rs.at[h, i, core], space_peer(dest))

    def cot_arrival(h, i, e):
        return remote(outbuf.at[h, i, e], inbuf.at[h, i, e], cot_ss.at[h, i, e], cot_rs.at[h, i, e], sibling)

    def is_own(i, c):
        return (i == last) & (c == core)

    for h in range(PARTS):
        @pl.loop(0, ns)
        def _(t):
            i, c = t // 2, lax.rem(t, 2)

            @pl.when(jnp.logical_not(is_own(i, c)))
            def _():
                cot_copy(h, i, c).start()

        inbuf[h, last, core] = outbuf[h, last, core]

    row = lax.broadcasted_iota(jnp.int32, (BV, channels), 0)
    by = lax.rem(row // 4, 4)
    bz = lax.rem(row, 4)
    keep = (by > 0, by < 3, bz > 0, bz < 3)
    own_shift = (4, 60, 1, 63)
    side_shift = (52, 12, 61, 3)

    @pl.loop(0, slots)
    def _(b):
        blk = feat[b]
        wide = blk.astype(F32)
        taps[b, :, 0:channels] = blk
        taps[b, 16:64, channels : 2 * channels] = blk[0:48]
        taps[b, 0:48, 2 * channels : 3 * channels] = blk[16:64]
        for k in range(4):
            n = jnp.minimum(nbr_s[0, b, 2 + k], slots)
            side = feat[n].astype(F32)
            tap = jnp.where(
                keep[k], pltpu.roll(wide, own_shift[k], 0), pltpu.roll(side, side_shift[k], 0)
            )
            taps[b, :, (3 + k) * channels : (4 + k) * channels] = tap.astype(BF16)

    halo_right.wait_recv()
    halo_left.wait_recv()

    @pl.loop(0, slots)
    def _(b):
        nm = jnp.minimum(nbr_s[0, b, 0], 2 * slots)
        np_ = nbr_s[0, b, 1]
        np_ = jnp.where(np_ < slots, np_, jnp.minimum(jnp.maximum(np_ - slots, slots), 2 * slots))
        taps[b, 0:16, channels : 2 * channels] = ext_m[nm]
        taps[b, 48:64, 2 * channels : 3 * channels] = ext_p[np_]

    @pl.loop(0, nz)
    def _(i):
        zs = lax.rem(z + offset(i), nz)
        for e in range(2):
            s = zs * 2 + e
            for k in range(7):
                cols = slice(k * channels, (k + 1) * channels)
                pair = jnp.concatenate(
                    [taps[send_s[0, 0, s, 0], :, cols], taps[send_s[0, 0, s, 1], :, cols]], 0
                )
                taps_t[i, cols, e * LANES : (e + 1) * LANES] = pair.T

    load_w.wait()
    live = counts_s[0, 0] * BV

    @pl.loop(0, slots // 4)
    def _(t):
        rows = taps[pl.ds(t * 4, 4)].reshape(4 * BV, taps_w)
        conv = jnp.dot(rows, w[...], preferred_element_type=F32)
        index = lax.broadcasted_iota(jnp.int32, (4 * BV, channels), 0) + t * (4 * BV)
        conv = jnp.where(index < live, conv, 0.0)
        vout[pl.ds(t * 4, 4)] = conv.astype(BF16).reshape(4, BV, channels)

    store_out = pltpu.make_async_copy(vout, out_hbm, local_sem.at[3])
    store_out.start()

    def grad_chunk(h, i):
        for e in range(2):
            if i == last:
                @pl.when(e != core)
                def _():
                    cot_arrival(h, i, e).wait_recv()
            else:
                cot_arrival(h, i, e).wait_recv()

        @pl.loop(0, 7)
        def _(m):
            rows = pl.ds(pl.multiple_of(m * channels, channels), channels)
            term = jnp.dot(
                taps_t[i, rows, :], inbuf[h, i].reshape(2 * LANES, LANES), preferred_element_type=F32
            )
            if i == 0:
                acc[h, rows, :] = term
            else:
                acc[h, rows, :] += term

    def half_rows(c):
        return pl.ds(pl.multiple_of(c * half, 16), half)

    def core_copy(h):
        return remote(core_out.at[h], core_in.at[h], core_ss.at[h], core_rs.at[h], sibling)

    def x_copy(h, d):
        return remote(x_out.at[h, d], x_in.at[h, d], x_ss.at[h, d], x_rs.at[h, d], x_peer(d))

    def y_copy(h, d):
        return remote(y_out.at[h, d], y_in.at[h, d], y_ss.at[h, d], y_rs.at[h, d], y_peer(d))

    def z_copy(h, d):
        return remote(zbuf.at[h, z], zbuf.at[h, z], z_ss.at[h, d], z_rs.at[h, d], z_peer(d))

    def z_arrival(h, d):
        zs = lax.rem(z - d + nz, nz)
        return remote(zbuf.at[h, zs], zbuf.at[h, zs], z_ss.at[h, d], z_rs.at[h, d], z_peer(d))

    def y_rows(v):
        return pl.ds(pl.multiple_of(v * yr, 16), yr)

    def yg_copy(h, d):
        mine = ybuf.at[h, y_rows(y)]
        return remote(mine, mine, yg_ss.at[h, d], yg_rs.at[h, d], y_peer(d))

    def yg_arrival(h, d):
        theirs = ybuf.at[h, y_rows(lax.rem(y - d + ny, ny))]
        return remote(theirs, theirs, yg_ss.at[h, d], yg_rs.at[h, d], y_peer(d))

    def x_rows(v):
        return pl.ds(pl.multiple_of(core * half + v * xr, 16), xr)

    def xg_copy(h, d):
        mine = cbuf.at[h, x_rows(x)]
        return remote(mine, mine, xg_ss.at[h, d], xg_rs.at[h, d], x_peer(d))

    def xg_arrival(h, d):
        theirs = cbuf.at[h, x_rows(lax.rem(x - d + nx, nx))]
        return remote(theirs, theirs, xg_ss.at[h, d], xg_rs.at[h, d], x_peer(d))

    def cg_copy(h):
        mine = cbuf.at[h, half_rows(core)]
        return remote(mine, mine, cg_ss.at[h], cg_rs.at[h], sibling)

    def cg_arrival(h):
        theirs = cbuf.at[h, half_rows(1 - core)]
        return remote(theirs, theirs, cg_ss.at[h], cg_rs.at[h], sibling)

    def store_wg(h):
        return pltpu.make_async_copy(
            cbuf.at[h], wg_hbm.at[:, pl.ds(h * LANES, LANES)], local_sem.at[4 + h]
        )

    def sum_core(h):
        core_out[h] = acc[h, half_rows(1 - core), :].astype(BF16)
        core_copy(h).start()

    def sum_x(h):
        core_copy(h).wait_recv()
        acc[h, half_rows(core), :] += core_in[h].astype(F32)
        for d in range(1, nx):
            x_out[h, d] = acc[h, x_rows(lax.rem(x + d, nx)), :].astype(BF16)
            x_copy(h, d).start()

    def sum_y(h):
        total = acc[h, x_rows(x), :]
        for d in range(1, nx):
            x_copy(h, d).wait_recv()
            total += x_in[h, d].astype(F32)
        gx[0:xr, :] = total
        if xr < ny * yr:
            gx[xr : ny * yr, :] = jnp.zeros((ny * yr - xr, LANES), F32)
        for d in range(1, ny):
            y_out[h, d] = gx[y_rows(lax.rem(y + d, ny)), :].astype(BF16)
            y_copy(h, d).start()

    def sum_z(h):
        total = gx[y_rows(y), :]
        for d in range(1, ny):
            y_copy(h, d).wait_recv()
            total += y_in[h, d].astype(F32)
        zbuf[h, z] = total.astype(BF16)
        for d in range(1, nz):
            z_copy(h, d).start()

    def spread_y(h):
        for d in range(1, nz):
            z_arrival(h, d).wait_recv()
        total = zbuf[h, 0].astype(F32)
        for v in range(1, nz):
            total += zbuf[h, v].astype(F32)
        ybuf[h, y_rows(y), :] = (total * scale).astype(BF16)
        for d in range(1, ny):
            yg_copy(h, d).start()

    def spread_x(h):
        for d in range(1, ny):
            yg_arrival(h, d).wait_recv()
        cbuf[h, x_rows(x), :] = ybuf[h, 0:xr, :]
        for d in range(1, nx):
            xg_copy(h, d).start()

    def spread_core(h):
        for d in range(1, nx):
            xg_arrival(h, d).wait_recv()
        cg_copy(h).start()

    def finish(h):
        cg_arrival(h).wait_recv()
        store_wg(h).start()

    steps = (sum_core, sum_x, sum_y, sum_z, spread_y, spread_x, spread_core, finish)
    for i in range(nz):
        grad_chunk(0, i)
    sum_core(0)
    taken = 1
    for i in range(nz):
        grad_chunk(1, i)
        if i < nz - 1 and taken < len(steps):
            steps[taken](0)
            taken += 1
    sum_core(1)
    for step in steps[taken:]:
        step(0)
    for step in steps[1:]:
        step(1)

    halo_right.wait_send()
    halo_left.wait_send()
    for h in range(PARTS):
        @pl.loop(0, ns)
        def _(t):
            i, c = t // 2, lax.rem(t, 2)

            @pl.when(jnp.logical_not(is_own(i, c)))
            def _():
                cot_copy(h, i, c).wait_send()

        core_copy(h).wait_send()
        cg_copy(h).wait_send()
        for d in range(1, nx):
            x_copy(h, d).wait_send()
            xg_copy(h, d).wait_send()
        for d in range(1, ny):
            y_copy(h, d).wait_send()
            yg_copy(h, d).wait_send()
        for d in range(1, nz):
            z_copy(h, d).wait_send()
        store_wg(h).wait()
    store_out.wait()


def shards(dp_size, space_size, features, cotangent, weights, counts, neighbours, send_list, recv_list):
    slots, channels = features.shape[1], features.shape[-1]
    bal = cotangent.shape[1]
    ny = 1 << (dp_size.bit_length() // 2)
    nx = dp_size // ny
    nz = space_size // 2
    taps_w = 7 * channels
    half = taps_w // 2
    xr = half // nx
    yr = -(-xr // (16 * ny)) * 16
    scale = 1.0 / math.sqrt(dp_size * space_size * bal * BV)
    dma = pltpu.SemaphoreType.DMA
    vmem = pltpu.VMEM
    smem_spec = pl.BlockSpec(memory_space=pltpu.SMEM)
    any_spec = pl.BlockSpec(memory_space=pl.ANY)
    macs = 2 * slots * BV * taps_w * channels
    voxel_out, weight_grad = pl.pallas_call(
        functools.partial(kernel, (nx, ny, nz, slots, bal, channels, scale)),
        out_shape=(
            jax.ShapeDtypeStruct((slots, BV, channels), BF16),
            jax.ShapeDtypeStruct((taps_w, channels), BF16),
        ),
        in_specs=[any_spec] * 3 + [smem_spec] * 4,
        out_specs=(any_spec, any_spec),
        scratch_shapes=[
            vmem((bal, BV, channels), BF16),
            vmem((slots + 1, BV, channels), BF16),
            vmem((taps_w, channels), BF16),
            vmem((2 * slots + 1, 16, channels), BF16),
            vmem((2 * slots + 1, 16, channels), BF16),
            vmem((slots + 1, BV, taps_w), BF16),
            vmem((nz, taps_w, 2 * LANES), BF16),
            vmem((slots, BV, channels), BF16),
            vmem((PARTS, nz, 2, 2 * BV, LANES), BF16),
            vmem((PARTS, nz, 2, 2 * BV, LANES), BF16),
            vmem((PARTS, taps_w, LANES), F32),
            vmem((PARTS, half, LANES), BF16),
            vmem((PARTS, half, LANES), BF16),
            vmem((PARTS, nx, xr, LANES), BF16),
            vmem((PARTS, nx, xr, LANES), BF16),
            vmem((ny * yr, LANES), F32),
            vmem((PARTS, ny, yr, LANES), BF16),
            vmem((PARTS, ny, yr, LANES), BF16),
            vmem((PARTS, nz, yr, LANES), BF16),
            vmem((PARTS, ny * yr, LANES), BF16),
            vmem((PARTS, taps_w, LANES), BF16),
            dma((4 + PARTS,)),
            dma((2,)),
            dma((2,)),
            dma((PARTS, nz, 2)),
            dma((PARTS, nz, 2)),
            dma((PARTS,)),
            dma((PARTS,)),
            dma((PARTS, nx)),
            dma((PARTS, nx)),
            dma((PARTS, ny)),
            dma((PARTS, ny)),
            dma((PARTS, nz)),
            dma((PARTS, nz)),
            dma((PARTS, ny)),
            dma((PARTS, ny)),
            dma((PARTS, nx)),
            dma((PARTS, nx)),
            dma((PARTS,)),
            dma((PARTS,)),
        ],
        compiler_params=pltpu.CompilerParams(
            collective_id=0, has_side_effects=True, vmem_limit_bytes=48 * 1024 * 1024
        ),
        cost_estimate=pl.CostEstimate(flops=4 * macs, bytes_accessed=6 << 20, transcendentals=0),
    )(
        cotangent[0], features[0], weights.reshape(taps_w, channels),
        counts, neighbours, send_list, recv_list,
    )
    return voxel_out[None], weight_grad.reshape(7, channels, channels)


def solution(mesh):
    placed = (
        P("dp", "space", None, None),
        P("dp", "space", None, None),
        P(),
        P("dp", "space"),
        P("dp", "space", None),
        P("dp", "space", None, None),
        P("dp", "space"),
    )
    return jax.shard_map(
        functools.partial(shards, mesh.shape["dp"], mesh.shape["space"]),
        mesh=mesh,
        in_specs=placed,
        out_specs=(P("dp", "space", None, None), P()),
        check_vma=False,
    )
```

time: 458 us -> 114 us (0.25)
  waiting for transfers between devices: 342 us -> 0 us
  Pallas kernels: 0 us -> 105 us
  local copies, waits for them, and re-layouts: 51.4 us -> 7.35 us
  starting transfers between devices: 25.4 us -> 0 us
  other arithmetic: 17.9 us -> 0 us
  between operations: 14.5 us -> 1.3 us
  matrix products: 5.57 us -> 0 us
    psum x1 -> x0, waiting for transfers between devices: 282 us -> none  [shards(): summed = lax.psum(grad_term, ('dp', 'space'))]
    pallas_call x0 -> x1, Pallas kernels: none -> 105 us  [shards(): pl.pallas_call(functools.partial(kernel, (nx, ny, nz, slots, bal, channel...]
    all_to_all x2 -> x0, waiting for transfers between devices: 59.8 us -> none  [the longest x1 59.8 us: shards(): lax.all_to_all(outgoing, 'space', split_axis=0, concat_axis=0, tiled=True)]
    all_to_all x2 -> x0, starting transfers between devices: 15.3 us -> none  [the longest x1 9.94 us: shards(): lax.all_to_all(outgoing, 'space', split_axis=0, concat_axis=0, tiled=True)]
    gather x8 -> x0, local copies, waits for them, and re-layouts: 14.3 us -> none  [the longest x6 8.56 us: gather_faces(): lookup[link_rows[:, direction]].reshape(slot_count, 4, 4, channels)]
    another operation x26 -> x0, local copies, waits for them, and re-layouts: 14 us -> none  [the longest x7 5.51 us: shifted_taps(): return jnp.stack(tap_list, 0).reshape(7, -1, channels)]
    concatenate x8 -> x0, other arithmetic: 13.5 us -> none  [the longest x1 2.84 us: gather_faces(): jnp.concatenate([planes[direction].reshape(slot_count, 16, channels), fro...]
    ppermute x2 -> x0, starting transfers between devices: 10.1 us -> none  [the longest x1 5.39 us: with_halo(): lax.ppermute(tail, axis, [(i, (i + 1) % count) for i in range(ends)])]
  transfers between devices with their start and end apart: 5 -> 0, of which waited for: 3 -> 0; matrix products, arithmetic and copies ran while one was open for 2% -> 0% of each run, Pallas kernels for 0% -> 0%
where the time goes in v1:
time: 114 us
  Pallas kernels  105 us (92%)
  local copies, waits for them, and re-layouts  7.35 us (6%)
  between operations  1.3 us (1%)
    pallas_call x1, Pallas kernels, shards(): pl.pallas_call(functools.partial(kernel, (nx, ny, nz, slots, bal, channel...  105 us
    unnamed x16, local copies, waits for them, and re-layouts  7.35 us

profile of v1, /device:TPU:1, one launch (start us, length us, event | category | flops | bytes accessed | tf_op | source)
XLA Modules:
  0.0 113.7 jit_solution(6350532708814792644)
XLA Ops:
  1.3 0.0 copy-start.5
  1.3 0.7 copy-done.5
  2.0 0.0 copy-start.4
  2.0 0.1 copy.10.send_s
  2.0 0.6 copy-done.4
  2.6 0.0 copy-start.3
  2.6 0.1 copy.9.nbr_s
  2.7 0.6 copy-done.3
  3.3 0.0 copy-start
  3.3 1.2 %copy-done = bf16[1,32,64,256]{3,2,1,0:T(8,128)(2,1)S(1)} copy-done((bf16[1,32,64,256]{3,2,1,0:T(8,128)(2,1)S(1)}, bf16[1,32,64,256]{3,2,1,0:T(8,128)(2,1)}, u32[]{:S(2)}) %copy-start) | copy-done | bytes 1048600
  4.5 0.0 copy-start.1
  4.5 1.2 %copy-done.1 = bf16[7,256,256]{2,1,0:T(8,128)(2,1)S(1)} copy-done((bf16[7,256,256]{2,1,0:T(8,128)(2,1)S(1)}, bf16[7,256,256]{2,1,0:T(8,128)(2,1)}, u32[]{:S(2)}) %copy-start.1) | copy-done | bytes 917528
  5.7 0.0 copy-start.2
  5.7 1.0 copy-done.2
  6.7 105.0 %shard_map.86 = (bf16[32,64,256]{2,1,0:T(8,128)(2,1)S(1)}, bf16[1792,256]{1,0:T(8,128)(2,1)S(1)}) custom-call(bf16[16,64,256]{2,1,0:T(8,128)(2,1)S(1)} %bitcast.9, bf16[32,64,256]{2,1,0:T(8,128)(2,1)S(1)} %bitcast.7, bf16[1792,256]{1,0:T(8,128)(2,1)S(1)} %bitcast.8, s32[1,1]{1,0:T(1,128)S(6)} %copy.13.counts_s, s32[1,32,6]{2,1,0:T(8,128)S(1)} %copy.9.nbr_s, ...), custom_call_target="tpu_custom_call" | custom-call | flops 7516192768 | bytes 6291456 | tf_op jit(solution)/shard_map/pallas_call | solution.py:396
  111.8 1.0 copy.14
  112.7 0.9 copy.15
Async XLA Ops:
  1.3 0.7 copy-start.5
  2.0 0.7 copy-start.4
  2.6 0.7 copy-start.3
  3.3 1.2 %copy-start = (bf16[1,32,64,256]{3,2,1,0:T(8,128)(2,1)S(1)}, bf16[1,32,64,256]{3,2,1,0:T(8,128)(2,1)}, u32[]{:S(2)}) copy-start(bf16[1,32,64,256]{3,2,1,0:T(8,128)(2,1)} %param.7) | copy-start | bytes 3145732
  4.5 1.2 %copy-start.1 = (bf16[7,256,256]{2,1,0:T(8,128)(2,1)S(1)}, bf16[7,256,256]{2,1,0:T(8,128)(2,1)}, u32[]{:S(2)}) copy-start(bf16[7,256,256]{2,1,0:T(8,128)(2,1)} %param.9) | copy-start | bytes 2752516
  5.7 1.0 copy-start.2

commit v2 on v1

--- a/solution.py
+++ b/solution.py
@@ -18,8 +18,9 @@
 
 def kernel(
     dims,
-    cot_hbm, feat_hbm, w_hbm, counts_s, nbr_s, send_s, recv_s,
+    cot_hbm, feat_hbm, w_hbm, counts_s, nbr_hbm, send_hbm, recv_hbm,
     out_hbm, wg_hbm,
+    nbr_s, send_s, recv_s,
     cot, feat, w, ext_m, ext_p, taps, taps_t, vout,
     outbuf, inbuf, acc,
     core_out, core_in, x_out, x_in, gx, y_out, y_in, zbuf, ybuf, cbuf,
@@ -32,7 +33,7 @@
     taps_w = 7 * channels
     half = taps_w // 2
     xr = half // nx
-    yr = gx.shape[0] // ny
+    yr = gx.shape[1] // ny
     dp = lax.axis_index("dp")
     me = lax.axis_index("space")
     x, y = dp // ny, dp % ny
@@ -74,6 +75,14 @@
     load_cot = pltpu.make_async_copy(cot_hbm, cot, local_sem.at[0])
     load_feat = pltpu.make_async_copy(feat_hbm, feat.at[pl.ds(0, slots)], local_sem.at[1])
     load_w = pltpu.make_async_copy(w_hbm, w, local_sem.at[2])
+    small = [
+        pltpu.make_async_copy(src, dst, local_sem.at[4 + PARTS + i])
+        for i, (src, dst) in enumerate(
+            ((recv_hbm, recv_s), (nbr_hbm, nbr_s), (send_hbm, send_s))
+        )
+    ]
+    for copy in small:
+        copy.start()
     load_cot.start()
     load_feat.start()
     load_w.start()
@@ -89,6 +98,8 @@
     ext_m[2 * slots] = jnp.zeros((16, channels), BF16)
     ext_p[2 * slots] = jnp.zeros((16, channels), BF16)
 
+    for copy in small:
+        copy.wait()
     load_cot.wait()
 
     @pl.loop(0, ns)
@@ -160,7 +171,7 @@
         taps[b, 16:64, channels : 2 * channels] = blk[0:48]
         taps[b, 0:48, 2 * channels : 3 * channels] = blk[16:64]
         for k in range(4):
-            n = jnp.minimum(nbr_s[0, b, 2 + k], slots)
+            n = jnp.minimum(nbr_s[2 + k, 0, b], slots)
             side = feat[n].astype(F32)
             tap = jnp.where(
                 keep[k], pltpu.roll(wide, own_shift[k], 0), pltpu.roll(side, side_shift[k], 0)
@@ -172,8 +183,8 @@
 
     @pl.loop(0, slots)
     def _(b):
-        nm = jnp.minimum(nbr_s[0, b, 0], 2 * slots)
-        np_ = nbr_s[0, b, 1]
+        nm = jnp.minimum(nbr_s[0, 0, b], 2 * slots)
+        np_ = nbr_s[1, 0, b]
         np_ = jnp.where(np_ < slots, np_, jnp.minimum(jnp.maximum(np_ - slots, slots), 2 * slots))
         taps[b, 0:16, channels : 2 * channels] = ext_m[nm]
         taps[b, 48:64, 2 * channels : 3 * channels] = ext_p[np_]
@@ -186,7 +197,7 @@
             for k in range(7):
                 cols = slice(k * channels, (k + 1) * channels)
                 pair = jnp.concatenate(
-                    [taps[send_s[0, 0, s, 0], :, cols], taps[send_s[0, 0, s, 1], :, cols]], 0
+                    [taps[send_s[0, 0, 0, s], :, cols], taps[send_s[0, 0, 1, s], :, cols]], 0
                 )
                 taps_t[i, cols, e * LANES : (e + 1) * LANES] = pair.T
 
@@ -204,25 +215,23 @@
     store_out = pltpu.make_async_copy(vout, out_hbm, local_sem.at[3])
     store_out.start()
 
-    def grad_chunk(h, i):
-        for e in range(2):
-            if i == last:
-                @pl.when(e != core)
-                def _():
+    def grad_places(h, first, end):
+        for i in range(first, end):
+            for e in range(2):
+                if i == last:
+                    @pl.when(e != core)
+                    def _():
+                        cot_arrival(h, i, e).wait_recv()
+                else:
                     cot_arrival(h, i, e).wait_recv()
-            else:
-                cot_arrival(h, i, e).wait_recv()
-
-        @pl.loop(0, 7)
-        def _(m):
-            rows = pl.ds(pl.multiple_of(m * channels, channels), channels)
-            term = jnp.dot(
-                taps_t[i, rows, :], inbuf[h, i].reshape(2 * LANES, LANES), preferred_element_type=F32
-            )
-            if i == 0:
-                acc[h, rows, :] = term
-            else:
-                acc[h, rows, :] += term
+        for m in range(7):
+            rows = slice(m * channels, (m + 1) * channels)
+            term = jnp.zeros((channels, LANES), F32) if first == 0 else acc[h, rows, :]
+            for i in range(first, end):
+                term += jnp.dot(
+                    taps_t[i, rows, :], inbuf[h, i].reshape(2 * LANES, LANES), preferred_element_type=F32
+                )
+            acc[h, rows, :] = term
 
     def half_rows(c):
         return pl.ds(pl.multiple_of(c * half, 16), half)
@@ -294,15 +303,15 @@
         for d in range(1, nx):
             x_copy(h, d).wait_recv()
             total += x_in[h, d].astype(F32)
-        gx[0:xr, :] = total
+        gx[h, 0:xr, :] = total
         if xr < ny * yr:
-            gx[xr : ny * yr, :] = jnp.zeros((ny * yr - xr, LANES), F32)
+            gx[h, xr : ny * yr, :] = jnp.zeros((ny * yr - xr, LANES), F32)
         for d in range(1, ny):
-            y_out[h, d] = gx[y_rows(lax.rem(y + d, ny)), :].astype(BF16)
+            y_out[h, d] = gx[h, y_rows(lax.rem(y + d, ny)), :].astype(BF16)
             y_copy(h, d).start()
 
     def sum_z(h):
-        total = gx[y_rows(y), :]
+        total = gx[h, y_rows(y), :]
         for d in range(1, ny):
             y_copy(h, d).wait_recv()
             total += y_in[h, d].astype(F32)
@@ -337,20 +346,16 @@
         store_wg(h).start()
 
     steps = (sum_core, sum_x, sum_y, sum_z, spread_y, spread_x, spread_core, finish)
-    for i in range(nz):
-        grad_chunk(0, i)
-    sum_core(0)
-    taken = 1
-    for i in range(nz):
-        grad_chunk(1, i)
-        if i < nz - 1 and taken < len(steps):
-            steps[taken](0)
-            taken += 1
-    sum_core(1)
-    for step in steps[taken:]:
+    lead = 3
+    grad_places(0, 0, nz)
+    for step in steps[:lead]:
         step(0)
-    for step in steps[1:]:
-        step(1)
+    grad_places(1, 0, nz // 2)
+    grad_places(1, nz // 2, nz)
+    for i in range(len(steps)):
+        steps[i](1)
+        if i + lead < len(steps):
+            steps[i + lead](0)
 
     halo_right.wait_send()
     halo_left.wait_send()
@@ -390,7 +395,7 @@
     scale = 1.0 / math.sqrt(dp_size * space_size * bal * BV)
     dma = pltpu.SemaphoreType.DMA
     vmem = pltpu.VMEM
-    smem_spec = pl.BlockSpec(memory_space=pltpu.SMEM)
+    smem = pltpu.SMEM
     any_spec = pl.BlockSpec(memory_space=pl.ANY)
     macs = 2 * slots * BV * taps_w * channels
     voxel_out, weight_grad = pl.pallas_call(
@@ -399,9 +404,12 @@
             jax.ShapeDtypeStruct((slots, BV, channels), BF16),
             jax.ShapeDtypeStruct((taps_w, channels), BF16),
         ),
-        in_specs=[any_spec] * 3 + [smem_spec] * 4,
+        in_specs=[any_spec] * 3 + [pl.BlockSpec(memory_space=smem)] + [any_spec] * 3,
         out_specs=(any_spec, any_spec),
         scratch_shapes=[
+            smem((6, 1, slots), jnp.int32),
+            smem((1, 1, 2, space_size), jnp.int32),
+            smem((1, bal), jnp.int32),
             vmem((bal, BV, channels), BF16),
             vmem((slots + 1, BV, channels), BF16),
             vmem((taps_w, channels), BF16),
@@ -417,13 +425,13 @@
             vmem((PARTS, half, LANES), BF16),
             vmem((PARTS, nx, xr, LANES), BF16),
             vmem((PARTS, nx, xr, LANES), BF16),
-            vmem((ny * yr, LANES), F32),
+            vmem((PARTS, ny * yr, LANES), F32),
             vmem((PARTS, ny, yr, LANES), BF16),
             vmem((PARTS, ny, yr, LANES), BF16),
             vmem((PARTS, nz, yr, LANES), BF16),
             vmem((PARTS, ny * yr, LANES), BF16),
             vmem((PARTS, taps_w, LANES), BF16),
-            dma((4 + PARTS,)),
+            dma((7 + PARTS,)),
             dma((2,)),
             dma((2,)),
             dma((PARTS, nz, 2)),
@@ -444,12 +452,12 @@
             dma((PARTS,)),
         ],
         compiler_params=pltpu.CompilerParams(
-            collective_id=0, has_side_effects=True, vmem_limit_bytes=48 * 1024 * 1024
+            collective_id=0, has_side_effects=True, vmem_limit_bytes=60 * 1024 * 1024
         ),
         cost_estimate=pl.CostEstimate(flops=4 * macs, bytes_accessed=6 << 20, transcendentals=0),
     )(
         cotangent[0], features[0], weights.reshape(taps_w, channels),
-        counts, neighbours, send_list, recv_list,
+        counts, neighbours.transpose(2, 0, 1), send_list.transpose(0, 1, 3, 2), recv_list,
     )
     return voxel_out[None], weight_grad.reshape(7, channels, channels)
 

time: 114 us -> 86.1 us (0.76)
  Pallas kernels: 105 us -> 81.3 us
  local copies, waits for them, and re-layouts: 7.35 us -> 3.31 us
    pallas_call x1, Pallas kernels: 105 us -> 81.3 us  [shards(): pl.pallas_call(functools.partial(kernel, (nx, ny, nz, slots, bal, channel...]
    unnamed x16 -> x4, local copies, waits for them, and re-layouts: 7.35 us -> 3.31 us
where the time goes in v2:
time: 86.1 us; the launch traced here: 85.9 us
  Pallas kernels  81.3 us (94%)
  local copies, waits for them, and re-layouts  3.31 us (4%)
  between operations  1.29 us (1%)
    pallas_call x1, Pallas kernels, shards(): pl.pallas_call(functools.partial(kernel, (nx, ny, nz, slots, bal, channel...  81.3 us
    unnamed x4, local copies, waits for them, and re-layouts  3.31 us

profile of v2, /device:TPU:1, one launch (start us, length us, event | category | flops | bytes accessed | tf_op | source)
XLA Modules:
  0.0 85.9 jit_solution(17191031262670147662)
XLA Ops:
  1.3 81.3 %shard_map.86 = (bf16[32,64,256]{2,1,0:T(8,128)(2,1)}, bf16[1792,256]{1,0:T(8,128)(2,1)}) custom-call(bf16[16,64,256]{2,1,0:T(8,128)(2,1)} %bitcast.11, bf16[32,64,256]{2,1,0:T(8,128)(2,1)} %bitcast.9, bf16[1792,256]{1,0:T(8,128)(2,1)} %bitcast.10, s32[1,1]{1,0:T(1,128)S(6)} %copy.11.counts_s, s32[6,1,32]{2,1,0:T(1,128)} %bitcast.12, ...), custom_call_target="tpu_custom_call" | custom-call | flops 7516192768 | bytes 6291456 | tf_op jit(solution)/shard_map/pallas_call | solution.py:401
  82.6 0.0 copy-start
  82.6 2.4 %copy.12 = bf16[1,32,64,256]{3,2,1,0:T(8,128)(2,1)} copy(bf16[1,32,64,256]{3,2,1,0:T(8,128)(2,1)} %bitcast.7) | data formatting | bytes 2097152
  85.0 0.0 copy-done
  85.0 0.9 %copy.13 = bf16[7,256,256]{2,1,0:T(8,128)(2,1)} copy(bf16[7,256,256]{2,1,0:T(8,128)(2,1)S(1)} %bitcast.8) | data formatting | bytes 1835008
Async XLA Ops:
  82.6 2.4 %copy-start = (bf16[1792,256]{1,0:T(8,128)(2,1)S(1)}, bf16[1792,256]{1,0:T(8,128)(2,1)}, u32[]{:S(2)}) copy-start(bf16[1792,256]{1,0:T(8,128)(2,1)} %get-tuple-element.5) | copy-start | bytes 2752516

commit v3 on v2

--- a/solution.py
+++ b/solution.py
@@ -23,7 +23,7 @@
     nbr_s, send_s, recv_s,
     cot, feat, w, ext_m, ext_p, taps, taps_t, vout,
     outbuf, inbuf, acc,
-    core_out, core_in, x_out, x_in, gx, y_out, y_in, zbuf, ybuf, cbuf,
+    core_out, core_in, x_out, x_in, gx, y_out, y_in, zbuf, cbuf,
     local_sem, halo_ss, halo_rs, cot_ss, cot_rs,
     core_ss, core_rs, x_ss, x_rs, y_ss, y_rs, z_ss, z_rs,
     yg_ss, yg_rs, xg_ss, xg_rs, cg_ss, cg_rs,
@@ -102,6 +102,36 @@
         copy.wait()
     load_cot.wait()
 
+    load_feat.wait()
+
+    @pl.loop(0, slots)
+    def _(b):
+        ext_m[b] = feat[b, 48:64, :]
+        ext_p[b] = feat[b, 0:16, :]
+
+    pl.semaphore_wait(barrier, ns - 1 + nx - 1 + ny - 1)
+
+    halo_right = remote(
+        ext_m.at[pl.ds(0, slots)], ext_m.at[pl.ds(slots, slots)], halo_ss.at[0], halo_rs.at[0],
+        space_peer(lax.rem(me + 1, ns)),
+    )
+    halo_left = remote(
+        ext_p.at[pl.ds(0, slots)], ext_p.at[pl.ds(slots, slots)], halo_ss.at[1], halo_rs.at[1],
+        space_peer(lax.rem(me + ns - 1, ns)),
+    )
+    halo_right.start()
+    halo_left.start()
+
+    def cot_copy(h, i, c):
+        dest = lax.rem(z - offset(i) + nz, nz) * 2 + c
+        return remote(outbuf.at[h, i, c], inbuf.at[h, i, core], cot_ss.at[h, i, c], cot_rs.at[h, i, core], space_peer(dest))
+
+    def cot_arrival(h, i, e):
+        return remote(outbuf.at[h, i, e], inbuf.at[h, i, e], cot_ss.at[h, i, e], cot_rs.at[h, i, e], sibling)
+
+    def is_own(i, c):
+        return (i == last) & (c == core)
+
     @pl.loop(0, ns)
     def _(t):
         i, c = t // 2, lax.rem(t, 2)
@@ -115,47 +145,11 @@
             for h in range(PARTS):
                 outbuf[h, i, c, pl.ds(place * BV, BV), :] = block[:, h * LANES : (h + 1) * LANES]
 
-    load_feat.wait()
-
-    @pl.loop(0, slots)
-    def _(b):
-        ext_m[b] = feat[b, 48:64, :]
-        ext_p[b] = feat[b, 0:16, :]
-
-    pl.semaphore_wait(barrier, ns - 1 + nx - 1 + ny - 1)
-
-    halo_right = remote(
-        ext_m.at[pl.ds(0, slots)], ext_m.at[pl.ds(slots, slots)], halo_ss.at[0], halo_rs.at[0],
-        space_peer(lax.rem(me + 1, ns)),
-    )
-    halo_left = remote(
-        ext_p.at[pl.ds(0, slots)], ext_p.at[pl.ds(slots, slots)], halo_ss.at[1], halo_rs.at[1],
-        space_peer(lax.rem(me + ns - 1, ns)),
-    )
-    halo_right.start()
-    halo_left.start()
-
-    def cot_copy(h, i, c):
-        dest = lax.rem(z - offset(i) + nz, nz) * 2 + c
-        return remote(outbuf.at[h, i, c], inbuf.at[h, i, core], cot_ss.at[h, i, c], cot_rs.at[h, i, core], space_peer(dest))
-
-    def cot_arrival(h, i, e):
-        return remote(outbuf.at[h, i, e], inbuf.at[h, i, e], cot_ss.at[h, i, e], cot_rs.at[h, i, e], sibling)
-
-    def is_own(i, c):
-        return (i == last) & (c == core)
-
-    for h in range(PARTS):
-        @pl.loop(0, ns)
-        def _(t):
-            i, c = t // 2, lax.rem(t, 2)
-
-            @pl.when(jnp.logical_not(is_own(i, c)))
-            def _():
-                cot_copy(h, i, c).start()
-
-        inbuf[h, last, core] = outbuf[h, last, core]
-
+        @pl.when(jnp.logical_not(is_own(i, c)))
+        def _():
+            cot_copy(0, i, c).start()
+
+    inbuf[0, last, core] = outbuf[0, last, core]
     row = lax.broadcasted_iota(jnp.int32, (BV, channels), 0)
     by = lax.rem(row // 4, 4)
     bz = lax.rem(row, 4)
@@ -215,7 +209,18 @@
     store_out = pltpu.make_async_copy(vout, out_hbm, local_sem.at[3])
     store_out.start()
 
-    def grad_places(h, first, end):
+    @pl.loop(0, ns)
+    def _(t):
+        i, c = t // 2, lax.rem(t, 2)
+
+        @pl.when(jnp.logical_not(is_own(i, c)))
+        def _():
+            cot_copy(0, i, c).wait_send()
+            cot_copy(1, i, c).start()
+
+    inbuf[1, last, core] = outbuf[1, last, core]
+
+    def await_places(h, first, end):
         for i in range(first, end):
             for e in range(2):
                 if i == last:
@@ -224,20 +229,27 @@
                         cot_arrival(h, i, e).wait_recv()
                 else:
                     cot_arrival(h, i, e).wait_recv()
+
+    def grad_places(h, first, end):
+        await_places(h, first, end)
         for m in range(7):
             rows = slice(m * channels, (m + 1) * channels)
-            term = jnp.zeros((channels, LANES), F32) if first == 0 else acc[h, rows, :]
-            for i in range(first, end):
-                term += jnp.dot(
-                    taps_t[i, rows, :], inbuf[h, i].reshape(2 * LANES, LANES), preferred_element_type=F32
-                )
-            acc[h, rows, :] = term
-
-    def half_rows(c):
-        return pl.ds(pl.multiple_of(c * half, 16), half)
-
-    def core_copy(h):
-        return remote(core_out.at[h], core_in.at[h], core_ss.at[h], core_rs.at[h], sibling)
+            acc[h, rows, :] = product(h, first, end, rows)
+
+    def product(h, first, end, rows):
+        term = None
+        for i in range(first, end):
+            part = jnp.dot(
+                taps_t[i, rows, :], inbuf[h, i].reshape(2 * LANES, LANES), preferred_element_type=F32
+            )
+            term = part if term is None else term + part
+        return term
+
+    def ring(n):
+        return sorted(range(1, n), key=lambda d: min(d, n - d))
+
+    def core_copy(h, d):
+        return remote(core_out.at[h, d], core_in.at[h, d], core_ss.at[h, d], core_rs.at[h, d], sibling)
 
     def x_copy(h, d):
         return remote(x_out.at[h, d], x_in.at[h, d], x_ss.at[h, d], x_rs.at[h, d], x_peer(d))
@@ -255,68 +267,85 @@
     def y_rows(v):
         return pl.ds(pl.multiple_of(v * yr, 16), yr)
 
+    whole = xr // yr
+
+    def piece(v, u, rows=yr):
+        return pl.ds(pl.multiple_of(core * half + v * xr + u * yr, 16), rows)
+
     def yg_copy(h, d):
-        mine = ybuf.at[h, y_rows(y)]
+        mine = cbuf.at[h, piece(x, y)]
         return remote(mine, mine, yg_ss.at[h, d], yg_rs.at[h, d], y_peer(d))
 
     def yg_arrival(h, d):
-        theirs = ybuf.at[h, y_rows(lax.rem(y - d + ny, ny))]
+        theirs = cbuf.at[h, piece(x, lax.rem(y - d + ny, ny))]
         return remote(theirs, theirs, yg_ss.at[h, d], yg_rs.at[h, d], y_peer(d))
 
-    def x_rows(v):
-        return pl.ds(pl.multiple_of(core * half + v * xr, 16), xr)
-
-    def xg_copy(h, d):
-        mine = cbuf.at[h, x_rows(x)]
-        return remote(mine, mine, xg_ss.at[h, d], xg_rs.at[h, d], x_peer(d))
-
-    def xg_arrival(h, d):
-        theirs = cbuf.at[h, x_rows(lax.rem(x - d + nx, nx))]
-        return remote(theirs, theirs, xg_ss.at[h, d], xg_rs.at[h, d], x_peer(d))
-
-    def cg_copy(h):
-        mine = cbuf.at[h, half_rows(core)]
-        return remote(mine, mine, cg_ss.at[h], cg_rs.at[h], sibling)
-
-    def cg_arrival(h):
-        theirs = cbuf.at[h, half_rows(1 - core)]
-        return remote(theirs, theirs, cg_ss.at[h], cg_rs.at[h], sibling)
+    def xg_copy(h, u, d):
+        mine = cbuf.at[h, piece(x, u)]
+        return remote(mine, mine, xg_ss.at[h, u, d], xg_rs.at[h, u, d], x_peer(d))
+
+    def xg_arrival(h, u, d):
+        theirs = cbuf.at[h, piece(lax.rem(x - d + nx, nx), u)]
+        return remote(theirs, theirs, xg_ss.at[h, u, d], xg_rs.at[h, u, d], x_peer(d))
+
+    def cg_copy(h, d):
+        mine = cbuf.at[h, piece(lax.rem(x - d + nx, nx), 0, xr)]
+        return remote(mine, mine, cg_ss.at[h, d], cg_rs.at[h, d], sibling)
+
+    def cg_arrival(h, d):
+        start = (1 - core) * half + lax.rem(x - d + nx, nx) * xr
+        theirs = cbuf.at[h, pl.ds(pl.multiple_of(start, 16), xr)]
+        return remote(theirs, theirs, cg_ss.at[h, d], cg_rs.at[h, d], sibling)
 
     def store_wg(h):
         return pltpu.make_async_copy(
             cbuf.at[h], wg_hbm.at[:, pl.ds(h * LANES, LANES)], local_sem.at[4 + h]
         )
 
-    def sum_core(h):
-        core_out[h] = acc[h, half_rows(1 - core), :].astype(BF16)
-        core_copy(h).start()
-
-    def sum_x(h):
-        core_copy(h).wait_recv()
-        acc[h, half_rows(core), :] += core_in[h].astype(F32)
-        for d in range(1, nx):
-            x_out[h, d] = acc[h, x_rows(lax.rem(x + d, nx)), :].astype(BF16)
-            x_copy(h, d).start()
+    def grad_x(h, first, begun):
+        await_places(h, first, nz)
+        order = ring(nx)[::-1] + [0]
+
+        def rows_of(c, d):
+            start = c * half + lax.rem(x + d, nx) * xr
+            return pl.ds(pl.multiple_of(start, 16), xr)
+
+        def total(c, d):
+            term = product(h, first, nz, rows_of(c, d))
+            return term + acc[h, rows_of(c, d), :] if begun else term
+
+        for d in order:
+            core_out[h, d] = total(1 - core, d).astype(BF16)
+            core_copy(h, d).start()
+        for d in order:
+            term = total(core, d)
+            core_copy(h, d).wait_recv()
+            term += core_in[h, d].astype(F32)
+            if d:
+                x_out[h, d] = term.astype(BF16)
+                x_copy(h, d).start()
+            else:
+                gx[h, 0:xr, :] = term
 
     def sum_y(h):
-        total = acc[h, x_rows(x), :]
-        for d in range(1, nx):
+        total = gx[h, 0:xr, :]
+        for d in ring(nx):
             x_copy(h, d).wait_recv()
             total += x_in[h, d].astype(F32)
         gx[h, 0:xr, :] = total
         if xr < ny * yr:
             gx[h, xr : ny * yr, :] = jnp.zeros((ny * yr - xr, LANES), F32)
-        for d in range(1, ny):
+        for d in ring(ny)[::-1]:
             y_out[h, d] = gx[h, y_rows(lax.rem(y + d, ny)), :].astype(BF16)
             y_copy(h, d).start()
 
     def sum_z(h):
         total = gx[h, y_rows(y), :]
-        for d in range(1, ny):
+        for d in ring(ny):
             y_copy(h, d).wait_recv()
             total += y_in[h, d].astype(F32)
         zbuf[h, z] = total.astype(BF16)
-        for d in range(1, nz):
+        for d in ring(nz)[::-1]:
             z_copy(h, d).start()
 
     def spread_y(h):
@@ -325,57 +354,81 @@
         total = zbuf[h, 0].astype(F32)
         for v in range(1, nz):
             total += zbuf[h, v].astype(F32)
-        ybuf[h, y_rows(y), :] = (total * scale).astype(BF16)
-        for d in range(1, ny):
-            yg_copy(h, d).start()
+
+        @pl.when(y < whole)
+        def _():
+            cbuf[h, piece(x, y), :] = (total * scale).astype(BF16)
+            for d in ring(ny)[::-1]:
+                yg_copy(h, d).start()
+            for d in ring(nx)[::-1]:
+                xg_copy(h, y, d).start()
 
     def spread_x(h):
-        for d in range(1, ny):
-            yg_arrival(h, d).wait_recv()
-        cbuf[h, x_rows(x), :] = ybuf[h, 0:xr, :]
-        for d in range(1, nx):
-            xg_copy(h, d).start()
+        for d in ring(ny):
+            u = lax.rem(y - d + ny, ny)
+
+            @pl.when(u < whole)
+            def _():
+                yg_arrival(h, d).wait_recv()
+                for v in ring(nx)[::-1]:
+                    xg_copy(h, u, v).start()
+        cg_copy(h, 0).start()
 
     def spread_core(h):
-        for d in range(1, nx):
-            xg_arrival(h, d).wait_recv()
-        cg_copy(h).start()
+        for d in ring(nx):
+            @pl.loop(0, whole)
+            def _(u):
+                xg_arrival(h, u, d).wait_recv()
+
+            cg_copy(h, d).start()
 
     def finish(h):
-        cg_arrival(h).wait_recv()
+        for d in [0] + ring(nx):
+            cg_arrival(h, d).wait_recv()
         store_wg(h).start()
 
-    steps = (sum_core, sum_x, sum_y, sum_z, spread_y, spread_x, spread_core, finish)
-    lead = 3
-    grad_places(0, 0, nz)
-    for step in steps[:lead]:
-        step(0)
+    grad_x(0, 0, False)
+    sum_y(0)
     grad_places(1, 0, nz // 2)
-    grad_places(1, nz // 2, nz)
-    for i in range(len(steps)):
-        steps[i](1)
-        if i + lead < len(steps):
-            steps[i + lead](0)
+    grad_x(1, nz // 2, True)
+    sum_z(0)
+    sum_y(1)
+    spread_y(0)
+    sum_z(1)
+    spread_x(0)
+    spread_y(1)
+    spread_core(0)
+    spread_x(1)
+    finish(0)
+    spread_core(1)
+    finish(1)
 
     halo_right.wait_send()
     halo_left.wait_send()
+    @pl.loop(0, ns)
+    def _(t):
+        i, c = t // 2, lax.rem(t, 2)
+
+        @pl.when(jnp.logical_not(is_own(i, c)))
+        def _():
+            cot_copy(PARTS - 1, i, c).wait_send()
+
     for h in range(PARTS):
-        @pl.loop(0, ns)
-        def _(t):
-            i, c = t // 2, lax.rem(t, 2)
-
-            @pl.when(jnp.logical_not(is_own(i, c)))
-            def _():
-                cot_copy(h, i, c).wait_send()
-
-        core_copy(h).wait_send()
-        cg_copy(h).wait_send()
+        for d in range(nx):
+            core_copy(h, d).wait_send()
+            cg_copy(h, d).wait_send()
         for d in range(1, nx):
             x_copy(h, d).wait_send()
-            xg_copy(h, d).wait_send()
+
+            @pl.loop(0, whole)
+            def _(u):
+                xg_copy(h, u, d).wait_send()
         for d in range(1, ny):
             y_copy(h, d).wait_send()
-            yg_copy(h, d).wait_send()
+
+            @pl.when(y < whole)
+            def _():
+                yg_copy(h, d).wait_send()
         for d in range(1, nz):
             z_copy(h, d).wait_send()
         store_wg(h).wait()
@@ -421,23 +474,22 @@
             vmem((PARTS, nz, 2, 2 * BV, LANES), BF16),
             vmem((PARTS, nz, 2, 2 * BV, LANES), BF16),
             vmem((PARTS, taps_w, LANES), F32),
-            vmem((PARTS, half, LANES), BF16),
-            vmem((PARTS, half, LANES), BF16),
+            vmem((PARTS, nx, xr, LANES), BF16),
+            vmem((PARTS, nx, xr, LANES), BF16),
             vmem((PARTS, nx, xr, LANES), BF16),
             vmem((PARTS, nx, xr, LANES), BF16),
             vmem((PARTS, ny * yr, LANES), F32),
             vmem((PARTS, ny, yr, LANES), BF16),
             vmem((PARTS, ny, yr, LANES), BF16),
             vmem((PARTS, nz, yr, LANES), BF16),
-            vmem((PARTS, ny * yr, LANES), BF16),
             vmem((PARTS, taps_w, LANES), BF16),
             dma((7 + PARTS,)),
             dma((2,)),
             dma((2,)),
             dma((PARTS, nz, 2)),
             dma((PARTS, nz, 2)),
-            dma((PARTS,)),
-            dma((PARTS,)),
+            dma((PARTS, nx)),
+            dma((PARTS, nx)),
             dma((PARTS, nx)),
             dma((PARTS, nx)),
             dma((PARTS, ny)),
@@ -446,10 +498,10 @@
             dma((PARTS, nz)),
             dma((PARTS, ny)),
             dma((PARTS, ny)),
+            dma((PARTS, ny, nx)),
+            dma((PARTS, ny, nx)),
             dma((PARTS, nx)),
             dma((PARTS, nx)),
-            dma((PARTS,)),
-            dma((PARTS,)),
         ],
         compiler_params=pltpu.CompilerParams(
             collective_id=0, has_side_effects=True, vmem_limit_bytes=60 * 1024 * 1024

time: 86.1 us -> 78.5 us (0.912)
  Pallas kernels: 81.3 us -> 73.8 us
    pallas_call x1, Pallas kernels: 81.3 us -> 73.8 us  [shards(): pl.pallas_call(functools.partial(kernel, (nx, ny, nz, slots, bal, channel...]
where the time goes in v3:
time: 78.5 us; the launch traced here: 78.4 us
  Pallas kernels  73.8 us (94%)
  local copies, waits for them, and re-layouts  3.31 us (4%)
  between operations  1.29 us (2%)
    pallas_call x1, Pallas kernels, shards(): pl.pallas_call(functools.partial(kernel, (nx, ny, nz, slots, bal, channel...  73.8 us
    unnamed x4, local copies, waits for them, and re-layouts  3.31 us

profile of v3, /device:TPU:1, one launch (start us, length us, event | category | flops | bytes accessed | tf_op | source)
XLA Modules:
  0.0 78.4 jit_solution(2654894177688760665)
XLA Ops:
  1.3 73.8 %shard_map.86 = (bf16[32,64,256]{2,1,0:T(8,128)(2,1)}, bf16[1792,256]{1,0:T(8,128)(2,1)}) custom-call(bf16[16,64,256]{2,1,0:T(8,128)(2,1)} %bitcast.11, bf16[32,64,256]{2,1,0:T(8,128)(2,1)} %bitcast.9, bf16[1792,256]{1,0:T(8,128)(2,1)} %bitcast.10, s32[1,1]{1,0:T(1,128)S(6)} %copy.11.counts_s, s32[6,1,32]{2,1,0:T(1,128)} %bitcast.12, ...), custom_call_target="tpu_custom_call" | custom-call | flops 7516192768 | bytes 6291456 | tf_op jit(solution)/shard_map/pallas_call | solution.py:454
  75.0 0.0 copy-start
  75.1 2.4 %copy.12 = bf16[1,32,64,256]{3,2,1,0:T(8,128)(2,1)} copy(bf16[1,32,64,256]{3,2,1,0:T(8,128)(2,1)} %bitcast.7) | data formatting | bytes 2097152
  77.4 0.0 copy-done
  77.4 0.9 %copy.13 = bf16[7,256,256]{2,1,0:T(8,128)(2,1)} copy(bf16[7,256,256]{2,1,0:T(8,128)(2,1)S(1)} %bitcast.8) | data formatting | bytes 1835008
Async XLA Ops:
  75.0 2.4 %copy-start = (bf16[1792,256]{1,0:T(8,128)(2,1)S(1)}, bf16[1792,256]{1,0:T(8,128)(2,1)}, u32[]{:S(2)}) copy-start(bf16[1792,256]{1,0:T(8,128)(2,1)} %get-tuple-element.5) | copy-start | bytes 2752516

commit v4 on v3

--- a/solution.py
+++ b/solution.py
@@ -302,6 +302,38 @@
             cbuf.at[h], wg_hbm.at[:, pl.ds(h * LANES, LANES)], local_sem.at[4 + h]
         )
 
+    def settle_sums(h):
+        for d in range(nx):
+            core_copy(h, d).wait_send()
+        for d in range(1, nx):
+            x_copy(h, d).wait_send()
+        for d in range(1, ny):
+            y_copy(h, d).wait_send()
+        for d in range(1, nz):
+            z_copy(h, d).wait_send()
+
+    def settle_gathers(h):
+        for d in range(1, nx):
+            @pl.loop(0, whole)
+            def _(u):
+                xg_copy(h, u, d).wait_send()
+        for d in range(1, ny):
+            @pl.when(y < whole)
+            def _():
+                yg_copy(h, d).wait_send()
+
+    def settle_places():
+        halo_right.wait_send()
+        halo_left.wait_send()
+
+        @pl.loop(0, ns)
+        def _(t):
+            i, c = t // 2, lax.rem(t, 2)
+
+            @pl.when(jnp.logical_not(is_own(i, c)))
+            def _():
+                cot_copy(PARTS - 1, i, c).wait_send()
+
     def grad_x(h, first, begun):
         await_places(h, first, nz)
         order = ring(nx)[::-1] + [0]
@@ -396,43 +428,47 @@
     spread_y(0)
     sum_z(1)
     spread_x(0)
+    settle_places()
+    settle_sums(0)
     spread_y(1)
     spread_core(0)
     spread_x(1)
     finish(0)
+    settle_sums(1)
+    settle_gathers(0)
+    for d in range(nx):
+        cg_copy(0, d).wait_send()
     spread_core(1)
+    settle_gathers(1)
     finish(1)
 
-    halo_right.wait_send()
-    halo_left.wait_send()
-    @pl.loop(0, ns)
-    def _(t):
-        i, c = t // 2, lax.rem(t, 2)
-
-        @pl.when(jnp.logical_not(is_own(i, c)))
-        def _():
-            cot_copy(PARTS - 1, i, c).wait_send()
-
+    for d in range(nx):
+        cg_copy(1, d).wait_send()
     for h in range(PARTS):
-        for d in range(nx):
-            core_copy(h, d).wait_send()
-            cg_copy(h, d).wait_send()
-        for d in range(1, nx):
-            x_copy(h, d).wait_send()
-
-            @pl.loop(0, whole)
-            def _(u):
-                xg_copy(h, u, d).wait_send()
-        for d in range(1, ny):
-            y_copy(h, d).wait_send()
-
-            @pl.when(y < whole)
-            def _():
-                yg_copy(h, d).wait_send()
-        for d in range(1, nz):
-            z_copy(h, d).wait_send()
         store_wg(h).wait()
     store_out.wait()
+
+
+def hand_over(out_in, wg_in, out, wg, out_mid, wg_mid, in_sem, out_sem):
+    pairs = []
+    for src, mid, dst in ((out_in, out_mid, out), (wg_in, wg_mid, wg)):
+        step = src.shape[0] // 4
+        for i in range(4):
+            part = pl.ds(i * step, step)
+            n = len(pairs)
+            pairs.append(
+                (
+                    pltpu.make_async_copy(src.at[part], mid.at[part], in_sem.at[n]),
+                    pltpu.make_async_copy(mid.at[part], dst.at[part], out_sem.at[n]),
+                )
+            )
+    for load, _ in pairs:
+        load.start()
+    for load, store in pairs:
+        load.wait()
+        store.start()
+    for _, store in pairs:
+        store.wait()
 
 
 def shards(dp_size, space_size, features, cotangent, weights, counts, neighbours, send_list, recv_list):
@@ -511,6 +547,22 @@
         cotangent[0], features[0], weights.reshape(taps_w, channels),
         counts, neighbours.transpose(2, 0, 1), send_list.transpose(0, 1, 3, 2), recv_list,
     )
+    voxel_out, weight_grad = pl.pallas_call(
+        hand_over,
+        out_shape=(
+            jax.ShapeDtypeStruct(voxel_out.shape, BF16),
+            jax.ShapeDtypeStruct(weight_grad.shape, BF16),
+        ),
+        in_specs=[any_spec] * 2,
+        out_specs=(any_spec, any_spec),
+        scratch_shapes=[
+            vmem(voxel_out.shape, BF16),
+            vmem(weight_grad.shape, BF16),
+            dma((8,)),
+            dma((8,)),
+        ],
+        compiler_params=pltpu.CompilerParams(vmem_limit_bytes=60 * 1024 * 1024),
+    )(voxel_out, weight_grad)
     return voxel_out[None], weight_grad.reshape(7, channels, channels)
 
 

time: 78.5 us -> 77.9 us (level)
  local copies, waits for them, and re-layouts: 3.31 us -> 0 us
  Pallas kernels: 73.8 us -> 76.4 us
    unnamed x4 -> x0, local copies, waits for them, and re-layouts: 3.31 us -> none
    pallas_call x0 -> x1, Pallas kernels: none -> 2.35 us  [shards(): pl.pallas_call(hand_over, out_shape=(jax.ShapeDtypeStruct(voxel_out.shape...]
where the time goes in v4:
time: 77.9 us; the launch traced here: 77.7 us
  Pallas kernels  76.4 us (98%)
  between operations  1.28 us (2%)
    pallas_call x1, Pallas kernels, shards(): pl.pallas_call(functools.partial(kernel, (nx, ny, nz, slots, bal, channel...  74.1 us
    pallas_call x1, Pallas kernels, shards(): pl.pallas_call(hand_over, out_shape=(jax.ShapeDtypeStruct(voxel_out.shape...  2.35 us

profile of v4, /device:TPU:1, one launch (start us, length us, event | category | flops | bytes accessed | tf_op | source)
XLA Modules:
  0.0 77.7 jit_solution(6046333685760362859)
XLA Ops:
  1.3 74.1 %shard_map.86 = (bf16[32,64,256]{2,1,0:T(8,128)(2,1)}, bf16[1792,256]{1,0:T(8,128)(2,1)}) custom-call(bf16[16,64,256]{2,1,0:T(8,128)(2,1)} %bitcast.11, bf16[32,64,256]{2,1,0:T(8,128)(2,1)} %bitcast.7, bf16[1792,256]{1,0:T(8,128)(2,1)} %bitcast.9, s32[1,1]{1,0:T(1,128)S(6)} %copy.9.counts_s, s32[6,1,32]{2,1,0:T(1,128)} %bitcast.12, ...), custom_call_target="tpu_custom_call" | custom-call | flops 7516192768 | bytes 6291456 | tf_op jit(solution)/shard_map/pallas_call | solution.py:490
  75.3 2.3 %shard_map.87 = (bf16[32,64,256]{2,1,0:T(8,128)(2,1)}, bf16[1792,256]{1,0:T(8,128)(2,1)}) custom-call(bf16[32,64,256]{2,1,0:T(8,128)(2,1)} %get-tuple-element.6.out_in, bf16[1792,256]{1,0:T(8,128)(2,1)} %get-tuple-element.7.wg_in), custom_call_target="tpu_custom_call" | custom-call | tf_op jit(solution)/shard_map/pallas_call | solution.py:550

commit v5 on v4

--- a/solution.py
+++ b/solution.py
@@ -88,8 +88,8 @@
     load_w.start()
 
     def offset(i):
-        k = (i + 1) // 2
-        return lax.rem(nz // 2 + k * (1 - 2 * lax.rem(i, 2)) + nz, nz)
+        k = i // 2 + 1
+        return lax.rem(k * (1 - 2 * lax.rem(i, 2)) + nz, nz) * (1 - i // (nz - 1))
 
     last = nz - 1
 
@@ -452,8 +452,8 @@
 def hand_over(out_in, wg_in, out, wg, out_mid, wg_mid, in_sem, out_sem):
     pairs = []
     for src, mid, dst in ((out_in, out_mid, out), (wg_in, wg_mid, wg)):
-        step = src.shape[0] // 4
-        for i in range(4):
+        step = src.shape[0] // 8
+        for i in range(8):
             part = pl.ds(i * step, step)
             n = len(pairs)
             pairs.append(
@@ -558,8 +558,8 @@
         scratch_shapes=[
             vmem(voxel_out.shape, BF16),
             vmem(weight_grad.shape, BF16),
-            dma((8,)),
-            dma((8,)),
+            dma((16,)),
+            dma((16,)),
         ],
         compiler_params=pltpu.CompilerParams(vmem_limit_bytes=60 * 1024 * 1024),
     )(voxel_out, weight_grad)

time: 77.9 us -> 77.7 us (level)
  no operation moved by 1% of the time
where the time goes in v5:
time: 77.7 us; the launch traced here: 77.5 us
  Pallas kernels  76.3 us (98%)
  between operations  1.28 us (2%)
    pallas_call x1, Pallas kernels, shards(): pl.pallas_call(functools.partial(kernel, (nx, ny, nz, slots, bal, channel...  73.7 us
    pallas_call x1, Pallas kernels, shards(): pl.pallas_call(hand_over, out_shape=(jax.ShapeDtypeStruct(voxel_out.shape...  2.53 us

profile of v5, /device:TPU:1, one launch (start us, length us, event | category | flops | bytes accessed | tf_op | source)
XLA Modules:
  0.0 77.5 jit_solution(5105950798771472903)
XLA Ops:
  1.3 73.7 %shard_map.86 = (bf16[32,64,256]{2,1,0:T(8,128)(2,1)}, bf16[1792,256]{1,0:T(8,128)(2,1)}) custom-call(bf16[16,64,256]{2,1,0:T(8,128)(2,1)} %bitcast.11, bf16[32,64,256]{2,1,0:T(8,128)(2,1)} %bitcast.7, bf16[1792,256]{1,0:T(8,128)(2,1)} %bitcast.9, s32[1,1]{1,0:T(1,128)S(6)} %copy.9.counts_s, s32[6,1,32]{2,1,0:T(1,128)} %bitcast.12, ...), custom_call_target="tpu_custom_call" | custom-call | flops 7516192768 | bytes 6291456 | tf_op jit(solution)/shard_map/pallas_call | solution.py:490
  75.0 2.5 %shard_map.87 = (bf16[32,64,256]{2,1,0:T(8,128)(2,1)}, bf16[1792,256]{1,0:T(8,128)(2,1)}) custom-call(bf16[32,64,256]{2,1,0:T(8,128)(2,1)} %get-tuple-element.6.out_in, bf16[1792,256]{1,0:T(8,128)(2,1)} %get-tuple-element.7.wg_in), custom_call_target="tpu_custom_call" | custom-call | tf_op jit(solution)/shard_map/pallas_call | solution.py:550
